TPU v7x, 32 devices: a whole 2x2x4 slice. The times are simulated.
32 devices in a mesh: visit: 8 (over y, x, core), ccd: 4 (over z).
Axes of the slice: x: 2, y: 2, z: 4, core: 2. Of those that a mesh axis runs over, the one named last changes fastest.
Arguments:
- raw_rows: bfloat16 [32, 4096, 128], P('visit', 'ccd')
- resample: bfloat16 [32, 128, 128], P('visit')
- slot_row: int32 [8, 4, 8, 128], P('visit', 'ccd'), may hold values from 0 to 4092, as said below
- tap_weight: float32 [4, 8, 4, 8, 128], P(None, 'visit', 'ccd'), may hold values from 0 to 1
- patch_id: int32 [8, 4, 8, 128], P('visit', 'ccd'), may hold values from 0 to 15
- live_mask: int32 [8, 4, 8, 128], P('visit', 'ccd'), may hold values 0 or 1
Outputs:
- offsets: float32 [32, 64], P('visit')
- background: float32 [512, 128], P(('visit', 'ccd'))
Inputs may be any that keep to these rules, and one draw needn't show every extreme that they name: `slot_row`: each value is v * 1024 + b with v below 4 and b at most 1020.
All inputs are finite; a program needn't handle non-finite values. No bound on the sum of `live_mask` on one device may be relied on, other than what follows from the above.
Results may differ from a plain program's by a relative error of at most 0.0041.
Values may be sent and summed in bfloat16 or wider, within the bound.
A program may use at most 64 MiB of HBM per device.

v0:
```python
import functools
import jax
import jax.numpy as jnp
import numpy as np
from jax import lax
from jax.experimental import pallas as pl
from jax.experimental.pallas import tpu as pltpu
from jax.sharding import PartitionSpec as P

ORDER = 8
TAPS = 4
P_DEV = 16
LANES = 128
ROW_BLOCK = 256

ridge_weight = 1.0

MESH = pl.DeviceIdType.MESH
F32 = jnp.float32
BF16 = jnp.bfloat16
NT = (((1,), (1,)), ((), ()))
NN = (((1,), (0,)), ((), ()))


def basis_constants(pixels, vis_local):
    coord = (2 * np.arange(pixels) + 1) / pixels - 1.0
    rows = [np.ones_like(coord), coord]
    for _ in range(2, ORDER):
        rows.append(2.0 * coord * rows[-1] - rows[-2])
    cheb = np.stack(rows)
    lam, vec = np.linalg.eigh(cheb @ cheb.T)
    used = np.arange(LANES) < vis_local * ORDER
    term = np.arange(LANES) % ORDER
    fold = (term[None] == np.arange(ORDER)[:, None]) * used
    unrot = vec[:, term] * used
    lam_lane = np.broadcast_to(lam[term] * used, (ORDER, LANES))
    wide = np.zeros((3 * ORDER + ORDER * ORDER, pixels))
    wide[:ORDER] = vec.T @ cheb
    wide[ORDER : 2 * ORDER, :LANES] = fold
    wide[2 * ORDER : 3 * ORDER, :LANES] = lam_lane
    wide[3 * ORDER :, :LANES] = np.repeat(unrot, ORDER, axis=0)
    return wide.astype(np.float32)


def dot(a, b, dims, precision=None):
    return lax.dot_general(a, b, dims, precision=precision, preferred_element_type=F32)


def split(x, parts):
    out = []
    for _ in range(parts):
        head = x.astype(BF16)
        out.append(head)
        x = x - head.astype(F32)
    return out


def wide_dot(a, b, dims):
    a_head, a_tail = split(a, 2)
    b_head, b_tail = split(b, 2)
    return dot(a_head, b_head, dims) + (dot(a_head, b_tail, dims) + dot(a_tail, b_head, dims))


def iota(shape, dim):
    return lax.broadcasted_iota(jnp.int32, shape, dim)


def kernel(
    n_v, n_c, vis_local,
    slot_hbm, tap_hbm, patch_hbm, live_hbm, const_hbm, raw_hbm, res_hbm,
    out_ref,
    slot_ref, tap_ref, patch_ref, live_ref, const_ref, raw_ref, res_ref, iscr, tscr, wscr, tw_ref, d_ref, s_ref, sext_ref, s1_ref,
    pa_ref, d_all, s_recv, m_recv, k_recv, pa_recv, o_recv, s1_recv,
    load_sem, ssend, srecv, asend, arecv, bsend, brecv, csend, crecv, ksend, krecv, gsend, grecv, dsend, drecv,
):
    vi, ci = lax.axis_index("visit"), lax.axis_index("ccd")
    rows = raw_ref.shape[1]
    slots = slot_ref.shape[3]
    npk = n_v * P_DEV
    nvb = vis_local * ORDER
    v_peer = lambda step: (lax.rem(vi + step, n_v), ci)
    c_peer = lambda step: (vi, lax.rem(ci + step, n_c))

    barrier = pltpu.get_barrier_semaphore()
    for step in range(1, n_v):
        pl.semaphore_signal(barrier, inc=1, device_id=v_peer(step), device_id_type=MESH)
    for step in range(1, n_c):
        pl.semaphore_signal(barrier, inc=1, device_id=c_peer(step), device_id_type=MESH)
    loads = []
    for src, dst in (
        (slot_hbm, slot_ref), (patch_hbm, patch_ref), (live_hbm, live_ref), (tap_hbm, tap_ref),
        (raw_hbm, raw_ref), (res_hbm, res_ref), (const_hbm, const_ref),
    ):
        loads.append(pltpu.make_async_copy(src, dst, load_sem.at[len(loads)]))
        loads[-1].start()

    def over_visits(src_of, dst, send, recv):
        copies = []
        for step in range(1, n_v):
            copy = pltpu.make_async_remote_copy(
                src_ref=src_of(step), dst_ref=dst.at[step],
                send_sem=send.at[step], recv_sem=recv.at[step],
                device_id=v_peer(step), device_id_type=MESH,
            )
            copy.start()
            copies.append(copy)
        return copies

    def over_ccd(buf, send, recv):
        copies = []
        for step in range(1, n_c):
            copy = pltpu.make_async_remote_copy(
                src_ref=buf.at[ci], dst_ref=buf.at[ci],
                send_sem=send.at[step], recv_sem=recv.at[ci],
                device_id=c_peer(step), device_id_type=MESH,
            )
            copy.start()
            copies.append(copy)
        return copies

    def total_over_ccd(buf, send, recv):
        for step in range(1, n_c):
            sender = lax.rem(ci + n_c - step, n_c)
            pltpu.make_async_remote_copy(
                src_ref=buf.at[sender], dst_ref=buf.at[sender],
                send_sem=send.at[step], recv_sem=recv.at[sender],
                device_id=c_peer(step), device_id_type=MESH,
            ).wait_recv()
        total = buf[0]
        for c in range(1, n_c):
            total = total + buf[c]
        return total

    for load in loads[:4]:
        load.wait()
    start = slot_ref[0, 0]
    vis = jnp.zeros_like(start)
    for v in range(1, vis_local):
        vis = vis + (start >= v * rows).astype(jnp.int32)
    base = start - vis * rows
    live = live_ref[0, 0] > 0
    patch = patch_ref[0, 0]
    iscr[0] = jnp.where(live, vis * P_DEV + patch, -1)
    iscr[1] = base
    iscr[2] = jnp.where(live, iota(start.shape, 0) * P_DEV + patch, -1)
    iscr[3] = jnp.where(live, vis, -1)
    coord = (2 * (ci * rows + base) + TAPS).astype(F32) / float(rows * n_c) - 1.0
    older, newer = jnp.ones_like(coord), coord
    for degree in range(2 * ORDER):
        tscr[:, degree, :] = older
        older, newer = newer, 2.0 * coord * newer - older

    out_ref[P_DEV:] = jnp.zeros_like(out_ref[P_DEV:])
    tw_ref[...] = jnp.zeros_like(tw_ref)
    d_ref[...] = jnp.zeros_like(d_ref)
    s_ref[...] = jnp.zeros_like(s_ref)
    row_at = iota((ROW_BLOCK, slots), 0).astype(F32).astype(BF16)
    group = 2 if n_v % 2 == 0 else 1
    hots = vis_local * P_DEV

    def chunk(step, carry):
        tops, terms, marks = [], [], []
        for part in range(group):
            j = step * group + part
            at = pl.ds(j, 1)
            vis_j = iscr[3, at, :]
            cheb = tscr[j]
            hot = jnp.where(iota((hots, slots), 0) == iscr[0, at, :], 1.0, 0.0).astype(BF16)
            cheb_v = jnp.concatenate(
                [jnp.where(vis_j == v, cheb[:ORDER], 0.0) for v in range(vis_local)], axis=0
            )
            tv = split(cheb_v, 3)
            empty = jnp.zeros_like(hot)
            tops.append(jnp.concatenate([hot if p == part else empty for p in range(group)], axis=0))
            terms.append(jnp.concatenate(tv[:2], axis=0))
            first = iscr[1, at, :]
            weights = [tap_ref[t, 0, 0, at, :].astype(BF16) for t in range(TAPS)]
            marks.append((first, [jnp.broadcast_to(w, (ROW_BLOCK, slots)) for w in weights]))
            member = jnp.where(iota((npk, slots), 0) == iscr[2, at, :], 1.0, 0.0).astype(BF16)
            design = dot(jnp.concatenate(tv, axis=0), member, NT)
            d_ref[...] += design[:nvb] + design[nvb : 2 * nvb] + design[2 * nvb :]
            of_visit = jnp.where((iota((LANES, slots), 0) >> 3) == vis_j, 1.0, 0.0).astype(BF16)
            sums = dot(jnp.concatenate(split(cheb, 3), axis=0), of_visit, NT)
            s_ref[...] += sums[: 2 * ORDER] + sums[2 * ORDER : 4 * ORDER] + sums[4 * ORDER :]
        lhs = jnp.concatenate(
            [jnp.concatenate(tops, axis=1), jnp.concatenate(terms, axis=1)], axis=0
        )
        for block in range(0, rows, ROW_BLOCK):
            wide = []
            for first, weights in marks:
                near = jnp.clip(first - block, -2 * TAPS, ROW_BLOCK + TAPS)
                taps = jnp.zeros((ROW_BLOCK, slots), BF16)
                for t in range(TAPS):
                    taps = jnp.where(row_at == (near + t).astype(F32).astype(BF16), weights[t], taps)
                wide.append(taps)
            prod = dot(lhs, jnp.concatenate(wide, axis=1), NT)
            for part in range(group):
                at = pl.ds(pl.multiple_of((step * group + part) * P_DEV, P_DEV), P_DEV)
                for v in range(vis_local):
                    low = part * hots + v * P_DEV
                    wscr[v, at, block : block + ROW_BLOCK] = prod[low : low + P_DEV].astype(BF16)
            low = group * hots
            tw_ref[:, block : block + ROW_BLOCK] += prod[low : low + nvb] + prod[low + nvb :]
        return carry

    lax.fori_loop(0, n_v // group, chunk, 0, unroll=2)

    pl.semaphore_wait(barrier, n_v + n_c - 2)
    s_recv[ci] = s_ref[...]
    sent_s = over_ccd(s_recv, ssend, srecv)
    d_all[0] = d_ref[...]
    sent_d = over_visits(lambda step: d_ref, d_all, dsend, drecv)

    for load in loads[4:]:
        load.wait()
    sums1 = jnp.zeros((npk, raw_ref.shape[2]), F32)
    row_sums = []
    for v in range(vis_local):
        tw = tw_ref[v * ORDER : (v + 1) * ORDER]
        tw_high = tw.astype(BF16).astype(F32)
        tw = jnp.concatenate([tw_high, tw - tw_high], axis=0).astype(BF16)
        by_patch = dot(jnp.concatenate([wscr[v], tw], axis=0), raw_ref[v], NN)
        by_term = by_patch[npk : npk + ORDER] + by_patch[npk + ORDER :]
        mixed = jnp.concatenate([by_patch[:npk], by_term, jnp.zeros_like(by_term)], axis=0)
        high, low = split(mixed, 2)
        warped = dot(high, res_ref[v], NN) + dot(low, res_ref[v], NN)
        sums1 = sums1 + warped[:npk]
        row_sums.append(warped[npk : npk + ORDER])
    s1_ref[...] = sums1
    cx = const_ref[:ORDER]
    design = d_ref[...]
    pa_ref[...] = wide_dot(cx, sums1, NT)
    sent_a = over_visits(lambda step: pa_ref, pa_recv, asend, arecv)

    def owner_rows(step):
        owner = lax.rem(vi + step, n_v)
        return s1_ref.at[pl.ds(pl.multiple_of(owner * P_DEV, P_DEV), P_DEV)]

    sent_g = over_visits(owner_rows, s1_recv, gsend, grecv)

    lane_visit = iota((ORDER, LANES), 1) >> 3

    def own_blocks(full):
        total = jnp.zeros((ORDER, LANES), F32)
        for v in range(vis_local):
            total = total + jnp.where(lane_visit == v, full[v * ORDER : (v + 1) * ORDER], 0.0)
        return total

    def repeat(x):
        return jnp.concatenate([x] * (LANES // ORDER), axis=0)

    warped_moment = own_blocks(wide_dot(jnp.concatenate(row_sums, axis=0), repeat(cx), NT))

    s_total = total_over_ccd(s_recv, ssend, srecv)
    s_ref[...] = s_total
    for q in range(2 * ORDER - 1):
        degree = abs(q - (ORDER - 1))
        sext_ref[q : q + 1] = s_ref[degree : degree + 1]
    lam = const_ref[2 * ORDER : 3 * ORDER, :LANES]
    sub = iota((ORDER, LANES), 0)
    system = []
    for b in range(ORDER):
        mean = 0.5 * (s_ref[b : b + ORDER] + sext_ref[ORDER - 1 - b : 2 * ORDER - 1 - b])
        system.append(lam * mean + jnp.where(sub == b, ridge_weight, 0.0))
    inverse = list(system)
    for k in range(ORDER):
        pivot = 1.0 / inverse[k][k : k + 1]
        off = jnp.where(sub == k, 0.0, inverse[k])
        for c in range(ORDER):
            if c != k:
                row = inverse[c][k : k + 1] * pivot
                inverse[c] = jnp.where(sub == k, row, inverse[c] - off * row)
        inverse[k] = jnp.where(sub == k, pivot, -off * pivot)

    def times(columns, x):
        total = columns[0] * x[0:1]
        for b in range(1, ORDER):
            total = total + columns[b] * x[b : b + 1]
        return total

    def solve(rhs):
        guess = times(inverse, rhs)
        return guess + times(inverse, rhs - times(system, guess))

    def spread(coefs):
        return [jnp.where(lane_visit == v, coefs, 0.0) for v in range(vis_local)]

    for copy in sent_d:
        copy.wait_recv()
    count = jnp.zeros((1, npk), F32)
    for step in range(n_v):
        for v in range(vis_local):
            count = count + d_all[step, v * ORDER : v * ORDER + 1]
    per_slot = 1.0 / (count + 1.0)
    design_all = d_all[...].reshape(n_v * nvb, npk)
    k_recv[ci] = wide_dot(design * per_slot, design_all, NT)

    for copy in sent_a:
        copy.wait_recv()
    projected = pa_ref[...]
    for step in range(1, n_v):
        projected = projected + pa_recv[step]
    m_recv[ci] = warped_moment - own_blocks(wide_dot(design, repeat(projected * per_slot), NT))
    sent_b = over_ccd(m_recv, bsend, brecv)
    sent_k = over_ccd(k_recv, ksend, krecv)
    moment = total_over_ccd(m_recv, bsend, brecv)
    o_recv[0] = solve(moment)

    sent_c = over_visits(lambda step: o_recv.at[0], o_recv, csend, crecv)
    k_total = total_over_ccd(k_recv, ksend, krecv)
    for copy in sent_c:
        copy.wait_recv()
    coefs = []
    for step in range(n_v):
        coefs += spread(o_recv[step])
    fold = const_ref[ORDER : 2 * ORDER, :LANES]
    coefs = wide_dot(fold, jnp.concatenate(coefs, axis=0), NT)
    moment = moment + lam * own_blocks(wide_dot(k_total, repeat(coefs), NT))
    terms = wide_dot(jnp.concatenate(spread(solve(moment)), axis=0), const_ref[3 * ORDER :, :LANES], NT)
    own_b = (iota(terms.shape, 1) & (ORDER - 1)) == (iota(terms.shape, 0) & (ORDER - 1))
    terms = jnp.where(own_b, terms, 0.0)
    for v in range(vis_local):
        out_ref[P_DEV + v : P_DEV + v + 1, : ORDER * ORDER] = jnp.sum(
            terms[v * ORDER : (v + 1) * ORDER], axis=0, keepdims=True
        )
    model = wide_dot(coefs, design_all, NN)

    mine = iota((P_DEV, npk), 1) == iota((P_DEV, npk), 0) + vi * P_DEV
    scale = jnp.where(mine, per_slot, 0.0)
    for copy in sent_g:
        copy.wait_recv()
    own = s1_ref[pl.ds(pl.multiple_of(vi * P_DEV, P_DEV), P_DEV)]
    for step in range(1, n_v):
        own = own + s1_recv[step]
    model_own = wide_dot(wide_dot(scale, model, NT), cx, NN)
    out_ref[:P_DEV] = own * jnp.sum(scale, axis=1, keepdims=True) - model_own

    for copy in sent_s + sent_d + sent_a + sent_g + sent_b + sent_k + sent_c:
        copy.wait_send()


def per_device(raw_rows, resample, slot_row, tap_weight, patch_id, live_mask):
    n_v, n_c = lax.axis_size("visit"), lax.axis_size("ccd")
    vis_local, rows, pixels = raw_rows.shape
    slots = slot_row.shape[3]
    npk, nvb = n_v * P_DEV, vis_local * ORDER
    consts = jnp.asarray(basis_constants(pixels, vis_local))
    vmem = pl.BlockSpec(memory_space=pltpu.VMEM)
    hbm = pl.BlockSpec(memory_space=pltpu.HBM)
    dma = pltpu.SemaphoreType.DMA
    packed = pl.pallas_call(
        functools.partial(kernel, n_v, n_c, vis_local),
        out_shape=pltpu.VMEM((P_DEV + 8 * (-(-vis_local // 8)), pixels), F32),
        in_specs=[hbm] * 7,
        out_specs=vmem,
        scratch_shapes=[
            pltpu.VMEM(slot_row.shape, jnp.int32),
            pltpu.VMEM(tap_weight.shape, F32),
            pltpu.VMEM(patch_id.shape, jnp.int32),
            pltpu.VMEM(live_mask.shape, jnp.int32),
            pltpu.VMEM(consts.shape, F32),
            pltpu.VMEM(raw_rows.shape, BF16),
            pltpu.VMEM(resample.shape, BF16),
            pltpu.VMEM((4, n_v, slots), jnp.int32),
            pltpu.VMEM((n_v, 2 * ORDER, slots), F32),
            pltpu.VMEM((vis_local, npk, rows), BF16),
            pltpu.VMEM((nvb, rows), F32),
            pltpu.VMEM((nvb, npk), F32),
            pltpu.VMEM((2 * ORDER, LANES), F32),
            pltpu.VMEM((2 * ORDER, LANES), F32),
            pltpu.VMEM((npk, pixels), F32),
            pltpu.VMEM((ORDER, npk), F32),
            pltpu.VMEM((n_v, nvb, npk), F32),
            pltpu.VMEM((n_c, 2 * ORDER, LANES), F32),
            pltpu.VMEM((n_c, ORDER, LANES), F32),
            pltpu.VMEM((n_c, nvb, n_v * nvb), F32),
            pltpu.VMEM((n_v, ORDER, npk), F32),
            pltpu.VMEM((n_v, ORDER, LANES), F32),
            pltpu.VMEM((n_v, P_DEV, pixels), F32),
            dma((7,)),
            dma((n_c,)), dma((n_c,)),
            dma((n_v,)), dma((n_v,)),
            dma((n_c,)), dma((n_c,)),
            dma((n_v,)), dma((n_v,)),
            dma((n_c,)), dma((n_c,)),
            dma((n_v,)), dma((n_v,)),
            dma((n_v,)), dma((n_v,)),
        ],
        compiler_params=pltpu.CompilerParams(
            collective_id=0, has_side_effects=True, vmem_limit_bytes=62 * 1024 * 1024
        ),
    )(slot_row, tap_weight, patch_id, live_mask, consts, raw_rows, resample)
    return (packed[P_DEV : P_DEV + vis_local, : ORDER * ORDER], packed[:P_DEV])


def solution(mesh):
    in_specs = (
        P("visit", "ccd", None),
        P("visit", None, None),
        P("visit", "ccd", None, None),
        P(None, "visit", "ccd", None, None),
        P("visit", "ccd", None, None),
        P("visit", "ccd", None, None),
    )
    out_specs = (P("visit", None), P(("visit", "ccd"), None))
    return jax.shard_map(
        per_device, mesh=mesh, in_specs=in_specs, out_specs=out_specs, check_vma=False
    )
```

profile of v0, /device:TPU:0, one launch (start us, length us, event | category | flops | bytes accessed | tf_op | source)
XLA Modules:
  0.0 20.8 jit_solution(4888816025879770550)
XLA Ops:
  0.6 18.9 %shard_map.86 = f32[24,128]{1,0:T(8,128)S(1)} custom-call(s32[1,1,8,128]{3,2,1,0:T(8,128)} %slot_hbm.1, f32[4,1,1,8,128]{4,3,2,1,0:T(8,128)} %tap_hbm.1, s32[1,1,8,128]{3,2,1,0:T(8,128)} %patch_hbm.1, s32[1,1,8,128]{3,2,1,0:T(8,128)} %live_hbm.1, f32[88,128]{1,0:T(8,128)} %constant.2.clone.const_hbm, bf16[4,1024,128]{2,1,0:T(8,128)(2,1)} %raw_hbm.1, ...), custom_call_target="tpu_custom_call" | custom-call | tf_op jit(solution)/shard_map/pallas_call | solution.py:351
  19.6 0.6 %slice.6 = f32[4,64]{1,0:T(4,128)} slice(f32[24,128]{1,0:T(8,128)S(1)} %shard_map.86), slice={[16:20], [0:64]} | slice | bytes 2048 | tf_op jit(solution)/shard_map/slice | solution.py:393
  20.2 0.6 %slice.7 = f32[16,128]{1,0:T(8,128)} slice(f32[24,128]{1,0:T(8,128)S(1)} %shard_map.86), slice={[0:16], [0:128]} | slice | bytes 16384 | tf_op jit(solution)/shard_map/slice | solution.py:393
where the time goes:
time: 20.9 us; the launch traced here: 20.8 us
  Pallas kernels  18.9 us (90%)
  local copies, waits for them, and re-layouts  1.18 us (6%)
  between operations  0.64 us (3%)
    pallas_call x1, Pallas kernels, per_device(): pl.pallas_call(functools.partial(kernel, n_v, n_c, vis_local), out_shape=...  18.9 us
    slice x2, local copies, waits for them, and re-layouts, per_device(): return (packed[P_DEV:P_DEV + vis_local, :ORDER * ORDER], packed[:P_DEV])  1.18 us

commit v1 on v0

--- a/solution.py
+++ b/solution.py
@@ -293,7 +293,6 @@
             count = count + d_all[step, v * ORDER : v * ORDER + 1]
     per_slot = 1.0 / (count + 1.0)
     design_all = d_all[...].reshape(n_v * nvb, npk)
-    k_recv[ci] = wide_dot(design * per_slot, design_all, NT)
 
     for copy in sent_a:
         copy.wait_recv()
@@ -302,11 +301,21 @@
         projected = projected + pa_recv[step]
     m_recv[ci] = warped_moment - own_blocks(wide_dot(design, repeat(projected * per_slot), NT))
     sent_b = over_ccd(m_recv, bsend, brecv)
+    k_recv[ci] = wide_dot(design * per_slot, design_all, NT)
     sent_k = over_ccd(k_recv, ksend, krecv)
+    mine = iota((P_DEV, npk), 1) == iota((P_DEV, npk), 0) + vi * P_DEV
+    scale = jnp.where(mine, per_slot, 0.0)
+    own_design = wide_dot(scale, design_all, NT)
     moment = total_over_ccd(m_recv, bsend, brecv)
     o_recv[0] = solve(moment)
 
     sent_c = over_visits(lambda step: o_recv.at[0], o_recv, csend, crecv)
+    for copy in sent_g:
+        copy.wait_recv()
+    own = s1_ref[pl.ds(pl.multiple_of(vi * P_DEV, P_DEV), P_DEV)]
+    for step in range(1, n_v):
+        own = own + s1_recv[step]
+    own = own * jnp.sum(scale, axis=1, keepdims=True)
     k_total = total_over_ccd(k_recv, ksend, krecv)
     for copy in sent_c:
         copy.wait_recv()
@@ -323,17 +332,7 @@
         out_ref[P_DEV + v : P_DEV + v + 1, : ORDER * ORDER] = jnp.sum(
             terms[v * ORDER : (v + 1) * ORDER], axis=0, keepdims=True
         )
-    model = wide_dot(coefs, design_all, NN)
-
-    mine = iota((P_DEV, npk), 1) == iota((P_DEV, npk), 0) + vi * P_DEV
-    scale = jnp.where(mine, per_slot, 0.0)
-    for copy in sent_g:
-        copy.wait_recv()
-    own = s1_ref[pl.ds(pl.multiple_of(vi * P_DEV, P_DEV), P_DEV)]
-    for step in range(1, n_v):
-        own = own + s1_recv[step]
-    model_own = wide_dot(wide_dot(scale, model, NT), cx, NN)
-    out_ref[:P_DEV] = own * jnp.sum(scale, axis=1, keepdims=True) - model_own
+    out_ref[:P_DEV] = own - wide_dot(wide_dot(own_design, coefs, NT), cx, NN)
 
     for copy in sent_s + sent_d + sent_a + sent_g + sent_b + sent_k + sent_c:
         copy.wait_send()

time: 20.9 us -> 20.5 us (0.981)
  Pallas kernels: 18.9 us -> 18.5 us
    pallas_call x1, Pallas kernels: 18.9 us -> 18.5 us  [per_device(): pl.pallas_call(functools.partial(kernel, n_v, n_c, vis_local), out_shape=...]
where the time goes in v1:
time: 20.5 us; the launch traced here: 20.3 us
  Pallas kernels  18.5 us (90%)
  local copies, waits for them, and re-layouts  1.18 us (6%)
  between operations  0.64 us (3%)
    pallas_call x1, Pallas kernels, per_device(): pl.pallas_call(functools.partial(kernel, n_v, n_c, vis_local), out_shape=...  18.5 us
    slice x2, local copies, waits for them, and re-layouts, per_device(): return (packed[P_DEV:P_DEV + vis_local, :ORDER * ORDER], packed[:P_DEV])  1.18 us

profile of v1, /device:TPU:0, one launch (start us, length us, event | category | flops | bytes accessed | tf_op | source)
XLA Modules:
  0.0 20.3 jit_solution(11576886627382959800)
XLA Ops:
  0.6 18.5 %shard_map.86 = f32[24,128]{1,0:T(8,128)S(1)} custom-call(s32[1,1,8,128]{3,2,1,0:T(8,128)} %slot_hbm.1, f32[4,1,1,8,128]{4,3,2,1,0:T(8,128)} %tap_hbm.1, s32[1,1,8,128]{3,2,1,0:T(8,128)} %patch_hbm.1, s32[1,1,8,128]{3,2,1,0:T(8,128)} %live_hbm.1, f32[88,128]{1,0:T(8,128)} %constant.2.clone.const_hbm, bf16[4,1024,128]{2,1,0:T(8,128)(2,1)} %raw_hbm.1, ...), custom_call_target="tpu_custom_call" | custom-call | tf_op jit(solution)/shard_map/pallas_call | solution.py:350
  19.2 0.6 %slice.6 = f32[4,64]{1,0:T(4,128)} slice(f32[24,128]{1,0:T(8,128)S(1)} %shard_map.86), slice={[16:20], [0:64]} | slice | bytes 2048 | tf_op jit(solution)/shard_map/slice | solution.py:392
  19.7 0.6 %slice.7 = f32[16,128]{1,0:T(8,128)} slice(f32[24,128]{1,0:T(8,128)S(1)} %shard_map.86), slice={[0:16], [0:128]} | slice | bytes 16384 | tf_op jit(solution)/shard_map/slice | solution.py:392

commit v2 on v1

--- a/solution.py
+++ b/solution.py
@@ -213,30 +213,20 @@
 
     for load in loads[4:]:
         load.wait()
-    sums1 = jnp.zeros((npk, raw_ref.shape[2]), F32)
-    row_sums = []
+    cx = const_ref[:ORDER]
+    cx_head, cx_tail = split(cx, 2)
+    back = [dot(cx_head, res_ref[v], NT) + dot(cx_tail, res_ref[v], NT) for v in range(vis_local)]
+    by_patch, by_row = [], []
     for v in range(vis_local):
         tw = tw_ref[v * ORDER : (v + 1) * ORDER]
         tw_high = tw.astype(BF16).astype(F32)
         tw = jnp.concatenate([tw_high, tw - tw_high], axis=0).astype(BF16)
-        by_patch = dot(jnp.concatenate([wscr[v], tw], axis=0), raw_ref[v], NN)
-        by_term = by_patch[npk : npk + ORDER] + by_patch[npk + ORDER :]
-        mixed = jnp.concatenate([by_patch[:npk], by_term, jnp.zeros_like(by_term)], axis=0)
-        high, low = split(mixed, 2)
-        warped = dot(high, res_ref[v], NN) + dot(low, res_ref[v], NN)
-        sums1 = sums1 + warped[:npk]
-        row_sums.append(warped[npk : npk + ORDER])
-    s1_ref[...] = sums1
-    cx = const_ref[:ORDER]
+        mixed = dot(jnp.concatenate([wscr[v], tw], axis=0), raw_ref[v], NN)
+        by_patch.append(mixed[:npk])
+        by_row.append(mixed[npk : npk + ORDER] + mixed[npk + ORDER :])
     design = d_ref[...]
-    pa_ref[...] = wide_dot(cx, sums1, NT)
+    pa_ref[...] = wide_dot(jnp.concatenate(back, axis=1), jnp.concatenate(by_patch, axis=1), NT)
     sent_a = over_visits(lambda step: pa_ref, pa_recv, asend, arecv)
-
-    def owner_rows(step):
-        owner = lax.rem(vi + step, n_v)
-        return s1_ref.at[pl.ds(pl.multiple_of(owner * P_DEV, P_DEV), P_DEV)]
-
-    sent_g = over_visits(owner_rows, s1_recv, gsend, grecv)
 
     lane_visit = iota((ORDER, LANES), 1) >> 3
 
@@ -249,7 +239,9 @@
     def repeat(x):
         return jnp.concatenate([x] * (LANES // ORDER), axis=0)
 
-    warped_moment = own_blocks(wide_dot(jnp.concatenate(row_sums, axis=0), repeat(cx), NT))
+    warped_moment = own_blocks(
+        jnp.concatenate([wide_dot(by_row[v], repeat(back[v]), NT) for v in range(vis_local)], axis=0)
+    )
 
     s_total = total_over_ccd(s_recv, ssend, srecv)
     s_ref[...] = s_total
@@ -306,6 +298,18 @@
     mine = iota((P_DEV, npk), 1) == iota((P_DEV, npk), 0) + vi * P_DEV
     scale = jnp.where(mine, per_slot, 0.0)
     own_design = wide_dot(scale, design_all, NT)
+    sums1 = jnp.zeros((npk, raw_ref.shape[2]), F32)
+    for v in range(vis_local):
+        high, low = split(by_patch[v], 2)
+        sums1 = sums1 + (dot(high, res_ref[v], NN) + dot(low, res_ref[v], NN))
+    s1_ref[...] = sums1
+
+    def owner_rows(step):
+        owner = lax.rem(vi + step, n_v)
+        return s1_ref.at[pl.ds(pl.multiple_of(owner * P_DEV, P_DEV), P_DEV)]
+
+    sent_g = over_visits(owner_rows, s1_recv, gsend, grecv)
+
     moment = total_over_ccd(m_recv, bsend, brecv)
     o_recv[0] = solve(moment)
 

time: 20.5 us -> 20.5 us (level)
  no operation moved by 1% of the time
where the time goes in v2:
time: 20.5 us; the launch traced here: 20.3 us
  Pallas kernels  18.4 us (90%)
  local copies, waits for them, and re-layouts  1.18 us (6%)
  between operations  0.64 us (3%)
    pallas_call x1, Pallas kernels, per_device(): pl.pallas_call(functools.partial(kernel, n_v, n_c, vis_local), out_shape=...  18.4 us
    slice x2, local copies, waits for them, and re-layouts, per_device(): return (packed[P_DEV:P_DEV + vis_local, :ORDER * ORDER], packed[:P_DEV])  1.18 us

profile of v2, /device:TPU:0, one launch (start us, length us, event | category | flops | bytes accessed | tf_op | source)
XLA Modules:
  0.0 20.3 jit_solution(13410591230114539616)
XLA Ops:
  0.6 18.4 %shard_map.86 = f32[24,128]{1,0:T(8,128)S(1)} custom-call(s32[1,1,8,128]{3,2,1,0:T(8,128)} %slot_hbm.1, f32[4,1,1,8,128]{4,3,2,1,0:T(8,128)} %tap_hbm.1, s32[1,1,8,128]{3,2,1,0:T(8,128)} %patch_hbm.1, s32[1,1,8,128]{3,2,1,0:T(8,128)} %live_hbm.1, f32[88,128]{1,0:T(8,128)} %constant.2.clone.const_hbm, bf16[4,1024,128]{2,1,0:T(8,128)(2,1)} %raw_hbm.1, ...), custom_call_target="tpu_custom_call" | custom-call | tf_op jit(solution)/shard_map/pallas_call | solution.py:354
  19.1 0.6 %slice.6 = f32[4,64]{1,0:T(4,128)} slice(f32[24,128]{1,0:T(8,128)S(1)} %shard_map.86), slice={[16:20], [0:64]} | slice | bytes 2048 | tf_op jit(solution)/shard_map/slice | solution.py:396
  19.7 0.6 %slice.7 = f32[16,128]{1,0:T(8,128)} slice(f32[24,128]{1,0:T(8,128)S(1)} %shard_map.86), slice={[0:16], [0:128]} | slice | bytes 16384 | tf_op jit(solution)/shard_map/slice | solution.py:396

commit v3 on v2

--- a/solution.py
+++ b/solution.py
@@ -203,7 +203,7 @@
             tw_ref[:, block : block + ROW_BLOCK] += prod[low : low + nvb] + prod[low + nvb :]
         return carry
 
-    lax.fori_loop(0, n_v // group, chunk, 0, unroll=2)
+    lax.fori_loop(0, n_v // group, chunk, 0, unroll=4)
 
     pl.semaphore_wait(barrier, n_v + n_c - 2)
     s_recv[ci] = s_ref[...]

time: 20.5 us -> 20.5 us (level)
  no operation moved by 1% of the time
where the time goes in v3:
time: 20.5 us; the launch traced here: 20.3 us
  Pallas kernels  18.4 us (90%)
  local copies, waits for them, and re-layouts  1.18 us (6%)
  between operations  0.64 us (3%)
    pallas_call x1, Pallas kernels, per_device(): pl.pallas_call(functools.partial(kernel, n_v, n_c, vis_local), out_shape=...  18.4 us
    slice x2, local copies, waits for them, and re-layouts, per_device(): return (packed[P_DEV:P_DEV + vis_local, :ORDER * ORDER], packed[:P_DEV])  1.18 us

profile of v3, /device:TPU:0, one launch (start us, length us, event | category | flops | bytes accessed | tf_op | source)
XLA Modules:
  0.0 20.3 jit_solution(6676367328818193736)
XLA Ops:
  0.6 18.4 %shard_map.86 = f32[24,128]{1,0:T(8,128)S(1)} custom-call(s32[1,1,8,128]{3,2,1,0:T(8,128)} %slot_hbm.1, f32[4,1,1,8,128]{4,3,2,1,0:T(8,128)} %tap_hbm.1, s32[1,1,8,128]{3,2,1,0:T(8,128)} %patch_hbm.1, s32[1,1,8,128]{3,2,1,0:T(8,128)} %live_hbm.1, f32[88,128]{1,0:T(8,128)} %constant.2.clone.const_hbm, bf16[4,1024,128]{2,1,0:T(8,128)(2,1)} %raw_hbm.1, ...), custom_call_target="tpu_custom_call" | custom-call | tf_op jit(solution)/shard_map/pallas_call | solution.py:354
  19.1 0.6 %slice.6 = f32[4,64]{1,0:T(4,128)} slice(f32[24,128]{1,0:T(8,128)S(1)} %shard_map.86), slice={[16:20], [0:64]} | slice | bytes 2048 | tf_op jit(solution)/shard_map/slice | solution.py:396
  19.7 0.6 %slice.7 = f32[16,128]{1,0:T(8,128)} slice(f32[24,128]{1,0:T(8,128)S(1)} %shard_map.86), slice={[0:16], [0:128]} | slice | bytes 16384 | tf_op jit(solution)/shard_map/slice | solution.py:396
